TPU v7x, 256 devices: a whole 4x4x8 slice. The times are simulated.
256 devices in a mesh: dp: 32 (over z, x_hi, core), fsdp: 8 (over y, x_lo).
Axes of the slice: x: 4 (x_hi: 2, x_lo: 2; x = x_hi * 2 + x_lo), y: 4, z: 8, core: 2. Of those that a mesh axis runs over, the one named last changes fastest.
Arguments:
- hidden: bfloat16 [256, 2, 128, 2560], P(('dp', 'fsdp')), may hold values from -6 to 6
- targets: bfloat16 [256, 2, 128, 2560], P(('dp', 'fsdp')), may hold values from -6 to 6
- lengths: int32 [256, 2], P(('dp', 'fsdp')), may hold values from 32 to 128
- prompt_group_index: int32 [256, 1], P(('dp', 'fsdp')), may hold values from 0 to 15
- input_norm_gain: float32 [2560], replicated, may hold values from 0.1 to 1.9
- frozen_weight: bfloat16 [2560, 3584], P('fsdp'), may hold values from -0.125 to 0.125
- adapter_down: bfloat16 [2560, 128], replicated, may hold values from -0.125 to 0.125
- adapter_up: bfloat16 [3072, 64], replicated, may hold values from -0.75 to 0.75
Outputs:
- pair_loss: float32 [256], P(('dp', 'fsdp'))
- grad_a: float32 [2560, 128], P('fsdp')
- grad_b: float32 [3072, 64], P('fsdp')
All inputs are finite; a program needn't handle non-finite values.
Results may differ from a plain program's by a relative error of at most 0.038.
Values may be sent and summed in bfloat16 or wider, within the bound.
A program may use at most 128 MiB of HBM per device.

v0:
```python
import jax
import jax.numpy as jnp
from jax import lax
from jax.sharding import PartitionSpec as P

QUERY_HEADS = 20
KEY_VALUE_HEADS = 4
HEAD_SIZE = 128
ADAPTER_RANK = 64
GROUPS = 16


EPS = 1e-05
BETA = 0.1
ADAPT_SCALE = 0.5


def normed_rows(rows, gain):
    values = rows.astype(jnp.float32)
    power = jnp.mean(values * values, -1, keepdims=True)
    return (values * lax.rsqrt(power + EPS) * gain).astype(jnp.bfloat16)


def seq_scores(query, keys, values, target, lengths):
    seqs, slots, qwidth = query.shape
    kvheads = keys.shape[-1] // HEAD_SIZE
    groups = qwidth // HEAD_SIZE // kvheads
    q_heads = query.reshape(seqs, slots, kvheads, groups, HEAD_SIZE)
    k_heads = keys.reshape(seqs, slots, kvheads, HEAD_SIZE)
    v_heads = values.reshape(seqs, slots, kvheads, HEAD_SIZE)
    scores = jnp.einsum(
        "nqhgd,nshd->nhgqs", q_heads, k_heads, preferred_element_type=jnp.float32
    ) * HEAD_SIZE ** (-0.5)
    places = jnp.arange(slots, dtype=jnp.int32)
    causal = places[None, :] <= places[:, None]
    inside = places[None, None, :] < lengths[:, None, None]
    allowed = (causal[None, :, :] & inside)[:, None, None, :, :]
    expo = jnp.where(allowed, jnp.exp(scores), jnp.float32(0.0))
    probs = (expo / jnp.sum(expo, -1, keepdims=True)).astype(jnp.bfloat16)
    attended = jnp.einsum("nhgqs,nshd->nqhgd", probs, v_heads, preferred_element_type=jnp.float32)
    attended = attended.astype(jnp.bfloat16).reshape(seqs, slots, qwidth)
    token = jnp.sum(attended.astype(jnp.float32) * target.astype(jnp.float32), -1) * qwidth ** (
        -0.5
    )
    valid = places[None, :] < lengths[:, None]
    return jnp.sum(jnp.where(valid, token, jnp.float32(0.0)), -1)


def split_base(base_offset):
    qwidth = QUERY_HEADS * HEAD_SIZE
    key_value_width = KEY_VALUE_HEADS * HEAD_SIZE
    return (
        base_offset[:, :qwidth],
        base_offset[:, qwidth : qwidth + key_value_width],
        base_offset[:, qwidth + key_value_width :],
    )


def contract_rows(left, right):
    return lax.dot_general(
        left, right, (((0,), (0,)), ((), ())), preferred_element_type=jnp.float32
    )


def pairwise_compute(normalized_input, base_offset, target, lengths, weight, first, second):
    seqs = target.shape[0]
    qwidth = QUERY_HEADS * HEAD_SIZE
    base_q, base_k, base_v = split_base(base_offset)
    keys = base_k.astype(jnp.bfloat16).reshape(seqs, -1, base_k.shape[-1])
    ref_scores = seq_scores(
        base_q.astype(jnp.bfloat16).reshape(seqs, -1, qwidth),
        keys,
        base_v.astype(jnp.bfloat16).reshape(seqs, -1, base_v.shape[-1]),
        target,
        lengths,
    )
    lowrank = jnp.dot(normalized_input, first, preferred_element_type=jnp.float32).astype(
        jnp.bfloat16
    )
    up_q = second[:qwidth]
    up_v = second[qwidth:]
    upper_q = jnp.dot(lowrank[:, :ADAPTER_RANK], up_q.T, preferred_element_type=jnp.float32)
    upper_v = jnp.dot(lowrank[:, ADAPTER_RANK:], up_v.T, preferred_element_type=jnp.float32)
    query = (base_q + ADAPT_SCALE * upper_q).astype(jnp.bfloat16)
    values = (base_v + ADAPT_SCALE * upper_v).astype(jnp.bfloat16)

    def scored(qrows, vrows):
        return seq_scores(
            qrows.reshape(seqs, -1, qwidth),
            keys,
            vrows.reshape(seqs, -1, vrows.shape[-1]),
            target,
            lengths,
        )

    pol_scores, pullback = jax.vjp(scored, query, values)
    pol_pairs = pol_scores.reshape(-1, 2)
    ref_pairs = ref_scores.reshape(-1, 2)
    margin = BETA * (pol_pairs[:, 0] - ref_pairs[:, 0] - (pol_pairs[:, 1] - ref_pairs[:, 1]))
    objective_loss = jax.nn.softplus(-margin)
    slope = -jax.nn.sigmoid(-margin) * weight * BETA
    cotangent = jnp.stack([slope, -slope], -1).reshape(-1)
    d_query, d_values = pullback(cotangent)
    grad_bq = ADAPT_SCALE * contract_rows(d_query, lowrank[:, :ADAPTER_RANK])
    grad_bv = ADAPT_SCALE * contract_rows(d_values, lowrank[:, ADAPTER_RANK:])
    low_q = jnp.dot(d_query, up_q, preferred_element_type=jnp.float32)
    low_v = jnp.dot(d_values, up_v, preferred_element_type=jnp.float32)
    d_low = (ADAPT_SCALE * jnp.concatenate([low_q, low_v], -1)).astype(jnp.bfloat16)
    gradient_leading = contract_rows(normalized_input, d_low)
    gradient_trailing = jnp.concatenate([grad_bq, grad_bv], 0)
    return (objective_loss, gradient_leading, gradient_trailing)


def body(
    hidden,
    targets,
    lengths,
    prompt_group_index,
    input_norm_gain,
    frozen_weight,
    adapter_down,
    adapter_up,
):
    pairs, _, slots, width = hidden.shape
    normalized_input = normed_rows(hidden.reshape(pairs * 2 * slots, width), input_norm_gain)
    full_rows = lax.all_gather(frozen_weight, "fsdp", axis=0, tiled=True)
    base_offset = jnp.dot(normalized_input, full_rows, preferred_element_type=jnp.float32)
    member = jax.nn.one_hot(prompt_group_index[:, 0], GROUPS, dtype=jnp.float32)
    counts = lax.psum(jnp.sum(member, 0), ("dp", "fsdp"))
    weight_list = 1.0 / (GROUPS * jnp.sum(member * counts[None, :], -1))
    sequence_target = targets.reshape(pairs * 2, slots, targets.shape[-1])
    sequence_length_list = lengths.reshape(pairs * 2)
    losses, gradient_leading, gradient_trailing = pairwise_compute(
        normalized_input,
        base_offset,
        sequence_target,
        sequence_length_list,
        weight_list,
        adapter_down,
        adapter_up,
    )
    shares = (
        lax.psum_scatter(
            gradient_leading.astype(jnp.bfloat16), "fsdp", scatter_dimension=0, tiled=True
        ).astype(jnp.float32),
        lax.psum_scatter(
            gradient_trailing.astype(jnp.bfloat16), "fsdp", scatter_dimension=0, tiled=True
        ).astype(jnp.float32),
    )
    summed = (
        lax.psum(shares[0].astype(jnp.bfloat16), "dp").astype(jnp.float32),
        lax.psum(shares[1].astype(jnp.bfloat16), "dp").astype(jnp.float32),
    )
    return (losses, summed[0], summed[1])


def solution(mesh):
    return jax.shard_map(
        body,
        mesh=mesh,
        in_specs=(
            P(("dp", "fsdp"), None, None, None),
            P(("dp", "fsdp"), None, None, None),
            P(("dp", "fsdp"), None),
            P(("dp", "fsdp"), None),
            P(),
            P("fsdp", None),
            P(),
            P(),
        ),
        out_specs=(P(("dp", "fsdp")), P("fsdp", None), P("fsdp", None)),
        check_vma=False,
    )
```

profile of v0, /device:TPU:1, one launch (start us, length us, event | category | flops | bytes accessed | tf_op | source)
XLA Modules:
  0.0 748.3 jit_solution(8098285301690568991)
XLA Ops:
  8.7 90.0 %psum.21 = f32[16]{0:T(128)S(1)} all-reduce(f32[16]{0:T(128)S(1)} %compare_convert_fusion), channel_id=1, replica_groups=mesh['dp'=32,'fsdp'=8] {'dp','fsdp'}, use_global_device_ids=true, to_apply=%region_7.8 | all-reduce | flops 16 | bytes 128 | tf_op jit(solution)/shard_map/psum | solution.py:129
  98.7 1.8 copy.46
  104.7 267.6 %all-gather.2.cloned.1.call-done = bf16[2560,3584]{1,0:T(8,128)(2,1)} async-done(((bf16[320,3584]{1,0:T(8,128)(2,1)}), bf16[2560,3584]{1,0:T(8,128)(2,1)}) %all-gather.2.cloned.1.call-update) | async-done | bytes 18350096 | tf_op jit(solution)/shard_map/all_gather | solution.py:126
  372.3 8.8 %fusion.79 = f32[256,3584]{1,0:T(8,128)S(1)} fusion(bf16[256,2560]{1,0:T(8,128)(2,1)S(1)} %fusion.13, bf16[2560,3584]{1,0:T(8,128)(2,1)} %all-gather.2.cloned.1.call-done), kind=kOutput, calls=%fused_computation.112 | convolution fusion | flops 4697620480 | bytes 23330816 | tf_op jit(solution)/shard_map/dot_general | solution.py:127
  382.1 1.6 fusion.1
  384.6 4.2 reshape.148
  389.8 2.5 reshape.149
  392.4 1.0 reshape_reshape.11
  393.4 1.0 reshape.127
  394.4 2.4 fusion.30
  396.9 1.7 fusion.16
  405.1 1.0 fusion.9
  406.2 2.2 fusion.21
  408.5 3.4 copy.55
  412.7 1.4 fusion.26
  414.1 1.2 fusion.50
  415.3 1.4 convolution_convert_fusion
  416.8 1.1 fusion.44
  418.4 1.2 copy.85
  419.7 34.7 %reduce-scatter.5.cloned.1.call-done = bf16[320,128]{1,0:T(8,128)(2,1)} async-done(((bf16[2560,128]{1,0:T(8,128)(2,1)}), bf16[320,128]{1,0:T(8,128)(2,1)}) %reduce-scatter.5.cloned.1.call-update) | async-done | bytes 81936 | tf_op jit(solution)/shard_map/reduce_scatter | solution.py:143
  454.5 43.4 %reduce-scatter.7.cloned.1.call-done = bf16[384,64]{1,0:T(8,128)(2,1)} async-done(((bf16[3072,64]{1,0:T(8,128)(2,1)}), bf16[384,64]{1,0:T(8,128)(2,1)}) %reduce-scatter.7.cloned.1.call-update) | async-done | bytes 49168
  498.9 128.4 %psum.23 = bf16[384,64]{0,1:T(8,128)(2,1)S(1)} all-reduce(bf16[384,64]{0,1:T(8,128)(2,1)S(1)} %copy.86), channel_id=1, replica_groups=mesh['dp'=32,'fsdp'=8] {'dp'}, use_global_device_ids=true, to_apply=%region_13.14 | all-reduce | flops 24576 | bytes 98304 | tf_op jit(solution)/shard_map/psum | solution.py:152
  628.0 111.2 %all-reduce.2.cloned.1.call-done = bf16[320,128]{1,0:T(8,128)(2,1)} async-done(((bf16[320,128]{1,0:T(8,128)(2,1)}), bf16[320,128]{1,0:T(8,128)(2,1)}) %all-reduce.2.cloned.1.call-update) | async-done | bytes 81936 | tf_op jit(solution)/shard_map/psum | solution.py:151
  739.1 1.6 convert_element_type.152
  (61 shorter events, 14.3 us)
Async XLA Ops:
  7.2 96.9 %copy-start = (bf16[2560,128]{1,0:T(8,128)(2,1)S(1)}, bf16[2560,128]{1,0:T(8,128)(2,1)}, u32[]{:S(2)}) copy-start(bf16[2560,128]{1,0:T(8,128)(2,1)} %param.14) | copy-start | bytes 1966084
  7.2 91.5 %copy-start.4 = (bf16[1,2,128,2560]{3,2,1,0:T(8,128)(2,1)S(1)}, bf16[1,2,128,2560]{3,2,1,0:T(8,128)(2,1)}, u32[]{:S(2)}) copy-start(bf16[1,2,128,2560]{3,2,1,0:T(8,128)(2,1)} %param.9) | copy-start | bytes 3932164
  7.2 94.6 %copy-start.2 = (bf16[1,2,128,2560]{3,2,1,0:T(8,128)(2,1)S(1)}, bf16[1,2,128,2560]{3,2,1,0:T(8,128)(2,1)}, u32[]{:S(2)}) copy-start(bf16[1,2,128,2560]{3,2,1,0:T(8,128)(2,1)} %param.8) | copy-start | bytes 3932164
  7.2 365.1 %all-gather.2.cloned.1.call-start = ((), (), s32[]{:S(2)}) async-start(), calls=%async_computation.2 | async-start | bytes 20643840 | tf_op jit(solution)/shard_map/all_gather | solution.py:126
  7.9 446.4 %reduce-scatter.5.cloned.1.call-start = ((), (), s32[]{:S(2)}) async-start(), calls=%async_computation.3 | async-start | bytes 737280 | tf_op jit(solution)/shard_map/reduce_scatter | solution.py:143
  98.7 3.5 copy-start.11
  98.7 5.0 copy-start.10
  104.6 279.1 %copy-start.6 = (bf16[256,128]{0,1:T(8,128)(2,1)}, bf16[256,128]{0,1:T(8,128)(2,1)S(1)}, u32[]{:S(2)}) copy-start(bf16[256,128]{0,1:T(8,128)(2,1)S(1)} %convolution_convert_fusion.4) | copy-start | bytes 196612
  381.0 1.1 copy-start.5
  392.4 4.5 copy-start.8
  394.4 2.4 copy-start.3
  396.9 1.8 copy-start.1
  405.1 1.1 copy-start.9
  412.7 4.0 copy-start.7
  416.7 81.2 %reduce-scatter.7.cloned.1.call-start = ((), (), s32[]{:S(2)}) async-start(), calls=%async_computation.5 | async-start | bytes 884736
  419.6 319.5 %all-reduce.2.cloned.1.call-start = ((), (), s32[]{:S(2)}) async-start(), calls=%async_computation.4 | async-start | bytes 163840 | tf_op jit(solution)/shard_map/psum | solution.py:151
Sparse Core Ops, SparseCore 0:
  9.8 362.3 all-gather.1
  416.8 37.5 reduce-scatter.4
  456.9 40.9 reduce-scatter.6
  500.6 238.5 all-reduce.1
where the time goes:
time: 750 us; the launch traced here: 748 us
  waiting for transfers between devices  458 us (61%)
  blocking collectives  218 us (29%)
  matrix products  27.8 us (4%)
  local copies, waits for them, and re-layouts  19.7 us (3%)
  between operations  19.3 us (3%)
    all_gather x1, waiting for transfers between devices, body(): full_rows = lax.all_gather(frozen_weight, 'fsdp', axis=0, tiled=True)  268 us
    psum x1, blocking collectives, body(): lax.psum(shares[1].astype(jnp.bfloat16), 'dp').astype(jnp.float32)  128 us
    psum x1, waiting for transfers between devices, body(): lax.psum(shares[0].astype(jnp.bfloat16), 'dp').astype(jnp.float32)  111 us
    psum x1, blocking collectives, body(): counts = lax.psum(jnp.sum(member, 0), ('dp', 'fsdp'))  90 us
    unnamed x5, waiting for transfers between devices  44.1 us
    reduce_scatter x1, waiting for transfers between devices, body(): lax.psum_scatter(gradient_leading.astype(jnp.bfloat16), 'fsdp', scatter_d...  34.7 us
  transfers between devices with their start and end apart: 4, of which 4 were waited for; matrix products, arithmetic and copies ran while one was open for 1% of the time, Pallas kernels for 0%

commit v1 on v0

v1 whole, which is shorter than its diff:
```python
import jax
import jax.numpy as jnp
from jax import lax
from jax.experimental import pallas as pl
from jax.experimental.pallas import tpu as pltpu
from jax.sharding import PartitionSpec as P

MODEL = 2560
HEAD = 128
RANK = 64
GROUPS = 16
EPS = 1e-05
BETA = 0.1
ADAPT_SCALE = 0.5

NZ, NX, NY = 8, 4, 4
SHARD = 320
HALF = 160
UNITS = 14
AHEAD0, AHEAD1, AHEAD2 = 4, 2, 1

MESH = pl.DeviceIdType.MESH
F32 = jnp.float32
BF16 = jnp.bfloat16


def mm(a, b):
    return lax.dot_general(a, b, (((1,), (0,)), ((), ())), preferred_element_type=F32)


def mm_nt(a, b):
    return lax.dot_general(a, b, (((1,), (1,)), ((), ())), preferred_element_type=F32)


def kernel(
    len_ref,
    grp_ref,
    gain_ref,
    hid_hbm,
    tgt_hbm,
    w_hbm,
    down_hbm,
    up_hbm,
    loss_ref,
    ga_ref,
    gb_ref,
    wbuf,
    hbuf,
    normed,
    normed_t,
    tbuf,
    down,
    up,
    lowq,
    lowv,
    low_t,
    kbuf,
    vpol,
    vref,
    mask,
    sacc,
    dvacc,
    dq_all,
    xsum,
    xrecv,
    meta,
    cnt,
    cbuf_y,
    cbuf_x,
    cbuf_z,
    red,
    red1,
    red2,
    ry,
    rx,
    rz,
    fin,
    wsem,
    lsem,
    y_send,
    y_recv,
    x_send,
    x_recv,
    d_send,
    d_recv,
    q_send,
    q_recv,
    c_send,
    c_recv,
    r_send,
    r_recv,
    g_send,
    g_recv,
):
    d = lax.axis_index("dp")
    f = lax.axis_index("fsdp")
    core = lax.rem(d, 2)
    xh = lax.rem(lax.div(d, 2), 2)
    z = lax.div(d, 4)
    par = lax.rem(f, 2)
    y = lax.div(f, 2)
    x = 2 * xh + par

    def dev(zz, xx, yy, cc):
        return (zz * 4 + lax.div(xx, 2) * 2 + cc, yy * 2 + lax.rem(xx, 2))

    def on_y(j):
        return dev(z, x, lax.rem(y + j, NY), core)

    def on_x(j):
        return dev(z, lax.rem(x + j, NX), y, core)

    def on_z(j):
        return dev(lax.rem(z + j, NZ), x, y, core)

    other = 1 - core
    mate = (d + 1 - 2 * core, f)

    def remote(src, dst, send, recv, target):
        return pltpu.make_async_remote_copy(
            src_ref=src,
            dst_ref=dst,
            send_sem=send,
            recv_sem=recv,
            device_id=target,
            device_id_type=MESH,
        )

    own_off = SHARD * f

    def shard_off(j):
        return SHARD * (2 * lax.rem(y + j, NY) + par)

    def rows(off, n):
        return pl.ds(pl.multiple_of(off, 32), n)

    def column(u):
        h = u // 7
        r = u % 7
        if r == 0:
            return MODEL + HEAD * (2 * core + h)
        if r == 1:
            return MODEL + 4 * HEAD + HEAD * (2 * core + h)
        return HEAD * (10 * core + 5 * h + r - 2)

    def lanes(off, n):
        return pl.ds(pl.multiple_of(off, HEAD), n)

    w_copies = []
    for u in range(UNITS):
        copy = pltpu.make_async_copy(
            w_hbm.at[:, lanes(column(u), HEAD)], wbuf.at[u, rows(own_off, SHARD), :], wsem.at[u]
        )
        copy.start()
        w_copies.append(copy)
        if u == 0:
            hid_copy = pltpu.make_async_copy(hid_hbm, hbuf, lsem.at[0])
            hid_copy.start()
    my_rows = rows(256 * core, 256)
    tgt_copy = pltpu.make_async_copy(
        tgt_hbm.at[:, lanes(1280 * core, 1280)], tbuf.at[my_rows, :], lsem.at[1]
    )
    tgt_copy.start()
    down_copy = pltpu.make_async_copy(down_hbm, down, lsem.at[2])
    down_copy.start()
    up_copy = pltpu.make_async_copy(up_hbm, up, lsem.at[3])
    up_copy.start()

    barrier = pltpu.get_barrier_semaphore()

    def greet(j, carry):
        pl.semaphore_signal(
            barrier, inc=1, device_id=(lax.rem(d + j, 32), f), device_id_type=MESH
        )
        return carry

    for j in (1, 2, 3):
        pl.semaphore_signal(barrier, inc=1, device_id=on_y(j), device_id_type=MESH)
    for j in (1, 3):
        pl.semaphore_signal(barrier, inc=1, device_id=on_x(j), device_id_type=MESH)
    lax.fori_loop(1, 32, greet, 0)

    lane = lax.broadcasted_iota(jnp.int32, (8, HEAD), 1)
    row = lax.broadcasted_iota(jnp.int32, (8, HEAD), 0)
    meta_own = jnp.where(
        row == 0,
        len_ref[0, 0].astype(F32),
        jnp.where(
            row == 1,
            len_ref[0, 1].astype(F32),
            jnp.where((row == 2) & (lane == grp_ref[0, 0]), F32(1.0), F32(0.0)),
        ),
    )
    meta[pl.ds(core, 1)] = meta_own[None]

    pl.semaphore_wait(barrier, 36)

    def piece(u, off, n):
        return wbuf.at[u, rows(off, n), :]

    def send_y(u, kind, off, n, target):
        ref = piece(u, off, n)
        remote(ref, ref, y_send.at[kind], y_recv.at[kind, u], target).start()

    def send_x(u, off):
        ref = piece(u, off, HALF)
        remote(ref, ref, x_send.at[0], x_recv.at[u], on_x(1)).start()

    def send_x_back(u, off):
        ref = piece(u, off + HALF, HALF)
        remote(ref, ref, x_send.at[1], x_recv.at[u], on_x(3)).start()

    def wait_y(u, kind, n):
        ref = wbuf.at[u, pl.ds(0, n), :]
        remote(ref, ref, y_send.at[kind], y_recv.at[kind, u], on_y(1)).wait_recv()

    def stage0(u):
        ref = wbuf.at[u, rows(own_off, SHARD), :]
        pltpu.make_async_copy(ref, ref, wsem.at[u]).wait()
        send_y(u, 0, own_off, SHARD, on_y(1))
        send_y(u, 1, own_off, SHARD, on_y(3))
        send_x(u, own_off)
        send_x_back(u, own_off)

    def stage1(u):
        wait_y(u, 0, SHARD)
        off = shard_off(3)
        send_y(u, 2, off, HALF, on_y(1))
        send_x(u, off)
        send_x_back(u, off)
        wait_y(u, 1, SHARD)
        off = shard_off(1)
        send_y(u, 3, off + HALF, HALF, on_y(3))
        send_x(u, off)
        send_x_back(u, off)

    def stage2(u):
        off = shard_off(2)
        wait_y(u, 2, HALF)
        send_x(u, off)
        wait_y(u, 3, HALF)
        send_x_back(u, off)

    def stage3(u):
        ref = wbuf.at[u, pl.ds(0, 8 * HALF), :]
        remote(ref, ref, x_send.at[0], x_recv.at[u], on_x(1)).wait_recv()

    def advance(u):
        @pl.when(u + AHEAD0 < UNITS)
        def _():
            stage0(u + AHEAD0)

        @pl.when(u + AHEAD1 < UNITS)
        def _():
            stage1(u + AHEAD1)

        @pl.when(u + AHEAD2 < UNITS)
        def _():
            stage2(u + AHEAD2)

        stage3(u)

    for u in range(AHEAD0):
        stage0(u)

    meta_copy = remote(
        meta.at[core], meta.at[core], d_send.at[0], d_recv.at[0], mate
    )
    meta_copy.start()
    tgt_remote = remote(
        tgt_hbm.at[:, lanes(1280 * other, 1280)],
        tbuf.at[my_rows, :],
        d_send.at[1],
        d_recv.at[1],
        mate,
    )
    tgt_remote.start()

    hid_copy.wait()
    gain = gain_ref[...]

    def norm_block(i, carry):
        values = hbuf[pl.ds(pl.multiple_of(32 * i, 32), 32), :].astype(F32)
        power = jnp.mean(values * values, -1, keepdims=True)
        out = (values * lax.rsqrt(power + EPS) * gain).astype(BF16)
        normed[rows(256 * core + 32 * i, 32), :] = out
        return carry

    lax.fori_loop(0, 8, norm_block, 0)
    normed_copy = remote(
        normed.at[my_rows, :], normed.at[my_rows, :], d_send.at[2], d_recv.at[2], mate
    )
    normed_copy.start()

    meta_copy.wait()
    cnt[0] = meta[0] + meta[1]

    def spread(step, count, place, buf):
        copies = []
        base = (0, 3, 6)[step]
        for j in range(1, count):
            copy = remote(
                cnt.at[step], buf.at[j - 1], c_send.at[base + j - 1], c_recv.at[base + j - 1], place(j)
            )
            copy.start()
            copies.append(copy)
        return copies

    def gathered(step, copies, buf):
        for copy in copies:
            copy.wait()
        cnt[step + 1] = cnt[step] + jnp.sum(buf[...], axis=0)

    copies_y = spread(0, NY, on_y, cbuf_y)
    stage1(0)

    down_copy.wait()
    up_copy.wait()
    key_at = lax.broadcasted_iota(jnp.int32, (HEAD, HEAD), 1)
    query_at = lax.broadcasted_iota(jnp.int32, (HEAD, HEAD), 0)
    for n in range(4):
        length = meta[n // 2, pl.ds(n % 2, 1), :]
        allowed = (key_at <= query_at) & (key_at.astype(F32) < length)
        mask[n] = jnp.where(allowed, F32(1.0), F32(0.0))
    tgt_copy.wait()
    tgt_remote.wait()
    for n in range(4):
        length = meta[n // 2, pl.ds(n % 2, 1), :]
        keep = query_at.astype(F32) < length
        for i in range(10):
            at = (pl.ds(HEAD * n, HEAD), pl.ds(HEAD * i, HEAD))
            tbuf[at] = jnp.where(keep, tbuf[at].astype(F32), F32(0.0)).astype(BF16)

    gathered(0, copies_y, cbuf_y)
    copies_x = spread(1, NX, on_x, cbuf_x)
    stage1(1)

    normed_copy.wait()
    low = mm(normed[...], down[...])
    lowq[...] = low[:, :RANK].astype(BF16)
    lowv[...] = low[:, RANK:].astype(BF16)
    for n in range(4):
        low_t[:, HEAD * n : HEAD * (n + 1)] = (
            low[HEAD * n : HEAD * (n + 1), :].astype(BF16).astype(F32).T
        )
    gathered(1, copies_x, cbuf_x)
    copies_z = spread(2, NZ, on_z, cbuf_z)
    stage2(0)

    sacc[...] = jnp.zeros_like(sacc)
    xsum[...] = jnp.zeros_like(xsum)

    def head_step(u, h, i):
        advance(u)
        qi = 5 * h + i
        base = mm(normed[...], wbuf[u])
        upq = up[rows(HEAD * (10 * core + qi), HEAD), :]
        upper = mm_nt(lowq[...], upq)
        qpol = (base + ADAPT_SCALE * upper).astype(BF16)
        qref = base.astype(BF16)
        grads = []
        for n in range(4):
            at = slice(HEAD * n, HEAD * (n + 1))
            keys = kbuf[h, at, :]
            values = vpol[h, at, :]
            both = jnp.concatenate([qpol[at], qref[at]], 0)
            scores = mm_nt(both, keys) * HEAD ** (-0.5)
            allowed = jnp.concatenate([mask[n], mask[n]], 0) > 0.0
            expo = jnp.where(allowed, jnp.exp(scores), F32(0.0))
            probs = expo * (1.0 / jnp.sum(expo, -1, keepdims=True))
            probs16 = probs.astype(BF16)
            pol = probs16[:HEAD]
            att_pol = mm(pol, values).astype(BF16).astype(F32)
            att_ref = mm(probs16[HEAD:], vref[h, at, :]).astype(BF16).astype(F32)
            target = tbuf[at, lanes(HEAD * qi, HEAD)]
            part = (att_pol - att_ref) * target.astype(F32)
            sacc[n] += jnp.sum(part.reshape(16, 8, HEAD), axis=0)
            d_probs = mm_nt(target, values)
            weighed = probs[:HEAD] * d_probs
            d_scores = weighed - probs[:HEAD] * jnp.sum(weighed, -1, keepdims=True)
            d_query = mm(d_scores.astype(BF16), keys).astype(BF16)
            grads.append(d_query)
            dvacc[at, :] += mm(probs[:HEAD].T.astype(BF16), target)
        d_query = jnp.concatenate(grads, 0)
        block = 10 * core + qi
        dq_all[block] = d_query
        remote(dq_all.at[block], dq_all.at[block], q_send.at[qi], q_recv.at[qi], mate).start()
        xsum[0:512, 0:RANK] += mm(d_query, upq)
        for j in range(2):
            at = lanes(HEAD * (2 * qi + j), HEAD)
            normed_t[at, :] = normed[:, at].T

    def group_step(h, carry):
        u = 7 * h
        advance(u)
        kbuf[h] = mm(normed[...], wbuf[u]).astype(BF16)
        advance(u + 1)
        base = mm(normed[...], wbuf[u + 1])
        upv = up[rows(MODEL + HEAD * (2 * core + h), HEAD), :]
        vref[h] = base.astype(BF16)
        vpol[h] = (base + ADAPT_SCALE * mm_nt(lowv[...], upv)).astype(BF16)
        dvacc[...] = jnp.zeros_like(dvacc)

        def inner(i, inner_carry):
            head_step(u + 2 + i, h, i)
            return inner_carry

        lax.fori_loop(0, 5, inner, 0)
        d_values = dvacc[...].astype(BF16)
        block = 20 + 2 * core + h
        dq_all[block] = d_values
        remote(
            dq_all.at[block], dq_all.at[block], q_send.at[10 + h], q_recv.at[10 + h], mate
        ).start()
        xsum[0:512, RANK:] += mm(d_values, upv)
        return carry

    lax.fori_loop(0, 2, group_step, 0)

    for n in range(4):
        xsum[512 + n : 513 + n, :] = jnp.sum(sacc[n], axis=0, keepdims=True)
    x_copy = remote(xsum, xrecv, d_send.at[3], d_recv.at[3], mate)
    x_copy.start()
    gathered(2, copies_z, cbuf_z)
    weights = []
    for c in range(2):
        count = jnp.sum(cnt[3, 2:3, :] * meta[c, 2:3, :], axis=-1, keepdims=True)
        weights.append(1.0 / (GROUPS * count))
    x_copy.wait()

    diffs = [
        jnp.sum(xsum[512 + n : 513 + n, :] + xrecv[512 + n : 513 + n, :], axis=-1, keepdims=True)
        * MODEL ** (-0.5)
        for n in range(4)
    ]
    coefs = []
    for c in range(2):
        margin = BETA * (diffs[2 * c] - diffs[2 * c + 1])
        loss = jnp.maximum(-margin, 0.0) + jnp.log1p(jnp.exp(-jnp.abs(margin)))
        slope = -(1.0 / (1.0 + jnp.exp(margin))) * weights[c] * BETA
        slope = slope * (ADAPT_SCALE * MODEL ** (-0.5))
        coefs += [slope, -slope]
        loss_ref[...] = loss if c == 0 else jnp.where(core == 1, loss, loss_ref[...])

    half_lane = lax.broadcasted_iota(jnp.int32, (1, HEAD), 1)
    half_row = lax.broadcasted_iota(jnp.int32, (HEAD, 1), 0)
    lane_scale = jnp.where(half_lane < RANK, F32(HEAD ** (-0.5)), F32(1.0))
    row_scale = jnp.where(half_row < RANK, F32(HEAD ** (-0.5)), F32(1.0))
    low_parts = []
    left_parts = []
    for n in range(4):
        at = slice(HEAD * n, HEAD * (n + 1))
        low_parts.append(((xsum[at, :] + xrecv[at, :]) * (lane_scale * coefs[n])).astype(BF16))
        low_t[:, at] = low_t[:, at] * (row_scale * coefs[n])
    d_low = jnp.concatenate(low_parts, 0)

    def share_a(j, carry):
        left = normed_t[rows(SHARD * j + HALF * core, HALF), :]
        red[j, 0:HALF, :] = mm(left, d_low).astype(BF16)
        return carry

    lax.fori_loop(0, 8, share_a, 0)

    def mate_blocks(i, carry):
        @pl.when(i < 10)
        def _():
            block = 10 * other + i
            remote(
                dq_all.at[10 * core + i], dq_all.at[block], q_send.at[i], q_recv.at[i], mate
            ).wait()

        @pl.when(i >= 10)
        def _():
            block = 20 + 2 * other + i - 10
            remote(
                dq_all.at[20 + 2 * core + i - 10], dq_all.at[block], q_send.at[i], q_recv.at[i], mate
            ).wait()

        return carry

    lax.fori_loop(0, 12, mate_blocks, 0)
    left_q = low_t[rows(32 * core, 32), :].astype(BF16)
    left_v = low_t[rows(RANK + 32 * core, 32), :].astype(BF16)
    for b in range(24):
        left = left_q if b < 20 else left_v
        at = HALF + 32 * (b % 3)
        red[b // 3, at : at + 32, :] = mm(left, dq_all[b]).astype(BF16)

    def exchange(step, count, place, source, buf):
        copies = []
        base = (0, 3, 6)[step]
        for j in range(1, count):
            copy = remote(
                source(j), buf.at[j - 1], r_send.at[base + j - 1], r_recv.at[base + j - 1], place(j)
            )
            copy.start()
            copies.append(copy)
        for copy in copies:
            copy.wait()

    exchange(0, NY, on_y, lambda j: red.at[pl.ds(2 * lax.rem(y + j, NY), 2)], ry)
    total = red[pl.ds(2 * y, 2)].astype(F32)
    for j in range(NY - 1):
        total += ry[j].astype(F32)
    red1[...] = total.astype(BF16)

    def x_part(j):
        xx = lax.rem(x + j, NX)
        return red1.at[lax.rem(xx, 2), rows(HEAD * lax.div(xx, 2), HEAD), :]

    exchange(1, NX, on_x, x_part, rx)
    total = red1[par, rows(HEAD * xh, HEAD), :].astype(F32)
    for j in range(NX - 1):
        total += rx[j].astype(F32)
    red2[...] = total.astype(BF16)

    def z_part(j):
        return red2.at[pl.ds(pl.multiple_of(16 * lax.rem(z + j, NZ), 16), 16), :]

    exchange(2, NZ, on_z, z_part, rz)
    total = red2[pl.ds(pl.multiple_of(16 * z, 16), 16), :].astype(F32)
    for j in range(NZ - 1):
        total += rz[j].astype(F32)
    mine = pl.ds(pl.multiple_of(HEAD * xh + 16 * z, 16), 16)
    fin[core, mine, :] = total.astype(BF16)

    def hand_out(j, carry):
        ref = fin.at[core, mine, :]
        remote(ref, ref, g_send.at[0], g_recv.at[0], (lax.rem(d + j, 32), f)).start()
        return carry

    lax.fori_loop(1, 32, hand_out, 0)
    whole = wbuf.at[0, pl.ds(0, 31 * 16), :]
    remote(whole, whole, g_send.at[0], g_recv.at[0], mate).wait()

    parts = [[], [], []]
    for c in range(2):
        ga_ref[HALF * c : HALF * (c + 1), :] = fin[c, 0:HALF, :].astype(F32)
        for i in range(3):
            at = HALF + 32 * i
            parts[i].append(fin[c, at : at + 32, :].astype(F32))
    for i in range(3):
        gb_ref[HEAD * i : HEAD * (i + 1), :] = jnp.concatenate(parts[i], 0).T

    whole = wbuf.at[:, pl.ds(0, SHARD), :]
    for kind in (0, 1):
        remote(whole, whole, y_send.at[kind], y_recv.at[kind, 0], mate).wait_send()
    whole = wbuf.at[:, pl.ds(0, HALF), :]
    for kind in (2, 3):
        remote(whole, whole, y_send.at[kind], y_recv.at[kind, 0], mate).wait_send()
    whole = wbuf.at[:, pl.ds(0, 4 * HALF), :]
    for kind in (0, 1):
        remote(whole, whole, x_send.at[kind], x_recv.at[0], mate).wait_send()


def fused(lengths, groups, gain, hidden, targets, weight, adapter_down, adapter_up):
    any_spec = pl.BlockSpec(memory_space=pl.ANY)
    smem = pl.BlockSpec(memory_space=pltpu.SMEM)
    vmem = pl.BlockSpec(memory_space=pltpu.VMEM)
    dma = pltpu.SemaphoreType.DMA
    return pl.pallas_call(
        kernel,
        out_shape=(
            jax.ShapeDtypeStruct((1, 1), F32),
            jax.ShapeDtypeStruct((SHARD, HEAD), F32),
            jax.ShapeDtypeStruct((3 * HEAD, RANK), F32),
        ),
        in_specs=[smem, smem, vmem, any_spec, any_spec, any_spec, any_spec, any_spec],
        out_specs=(vmem, vmem, vmem),
        scratch_shapes=[
            pltpu.VMEM((UNITS, MODEL, HEAD), BF16),
            pltpu.VMEM((256, MODEL), BF16),
            pltpu.VMEM((512, MODEL), BF16),
            pltpu.VMEM((MODEL, 512), BF16),
            pltpu.VMEM((512, 1280), BF16),
            pltpu.VMEM((MODEL, HEAD), BF16),
            pltpu.VMEM((3072, RANK), BF16),
            pltpu.VMEM((512, RANK), BF16),
            pltpu.VMEM((512, RANK), BF16),
            pltpu.VMEM((HEAD, 512), F32),
            pltpu.VMEM((2, 512, HEAD), BF16),
            pltpu.VMEM((2, 512, HEAD), BF16),
            pltpu.VMEM((2, 512, HEAD), BF16),
            pltpu.VMEM((4, HEAD, HEAD), F32),
            pltpu.VMEM((4, 8, HEAD), F32),
            pltpu.VMEM((512, HEAD), F32),
            pltpu.VMEM((24, 512, HEAD), BF16),
            pltpu.VMEM((520, HEAD), F32),
            pltpu.VMEM((520, HEAD), F32),
            pltpu.VMEM((2, 8, HEAD), F32),
            pltpu.VMEM((4, 8, HEAD), F32),
            pltpu.VMEM((NY - 1, 8, HEAD), F32),
            pltpu.VMEM((NX - 1, 8, HEAD), F32),
            pltpu.VMEM((NZ - 1, 8, HEAD), F32),
            pltpu.VMEM((8, 256, HEAD), BF16),
            pltpu.VMEM((2, 256, HEAD), BF16),
            pltpu.VMEM((HEAD, HEAD), BF16),
            pltpu.VMEM((NY - 1, 2, 256, HEAD), BF16),
            pltpu.VMEM((NX - 1, HEAD, HEAD), BF16),
            pltpu.VMEM((NZ - 1, 16, HEAD), BF16),
            pltpu.VMEM((2, 256, HEAD), BF16),
            dma((UNITS,)),
            dma((4,)),
            dma((4,)),
            dma((4, UNITS)),
            dma((2,)),
            dma((UNITS,)),
            dma((4,)),
            dma((4,)),
            dma((12,)),
            dma((12,)),
            dma((13,)),
            dma((13,)),
            dma((13,)),
            dma((13,)),
            dma((1,)),
            dma((1,)),
        ],
        compiler_params=pltpu.CompilerParams(
            collective_id=0, has_side_effects=True, vmem_limit_bytes=56 * 1024 * 1024
        ),
        cost_estimate=pl.CostEstimate(
            flops=8_000_000_000, bytes_accessed=8_000_000, transcendentals=1_400_000
        ),
    )(lengths, groups, gain, hidden, targets, weight, adapter_down, adapter_up)


def body(
    hidden,
    targets,
    lengths,
    prompt_group_index,
    input_norm_gain,
    frozen_weight,
    adapter_down,
    adapter_up,
):
    losses, grad_a, grad_b = fused(
        lengths,
        prompt_group_index,
        input_norm_gain.reshape(1, MODEL),
        hidden.reshape(256, MODEL),
        targets.reshape(256, MODEL),
        frozen_weight,
        adapter_down,
        adapter_up,
    )
    return (losses.reshape(1), grad_a, grad_b)


def solution(mesh):
    return jax.shard_map(
        body,
        mesh=mesh,
        in_specs=(
            P(("dp", "fsdp"), None, None, None),
            P(("dp", "fsdp"), None, None, None),
            P(("dp", "fsdp"), None),
            P(("dp", "fsdp"), None),
            P(),
            P("fsdp", None),
            P(),
            P(),
        ),
        out_specs=(P(("dp", "fsdp")), P("fsdp", None), P("fsdp", None)),
        check_vma=False,
    )
```

time: 750 us -> 128 us (0.17)
  waiting for transfers between devices: 458 us -> 0 us
  blocking collectives: 218 us -> 0 us
  Pallas kernels: 0 us -> 118 us
  matrix products: 27.8 us -> 0 us
  between operations: 19.3 us -> 3.06 us
  local copies, waits for them, and re-layouts: 19.7 us -> 6.75 us
    all_gather x1 -> x0, waiting for transfers between devices: 268 us -> none  [body(): full_rows = lax.all_gather(frozen_weight, 'fsdp', axis=0, tiled=True)]
    psum x2 -> x0, blocking collectives: 218 us -> none  [the longest x1 128 us: body(): lax.psum(shares[1].astype(jnp.bfloat16), 'dp').astype(jnp.float32)]
    pallas_call x0 -> x1, Pallas kernels: none -> 118 us  [fused(): pl.pallas_call(kernel, out_shape=(jax.ShapeDtypeStruct((1, 1), F32), jax....]
    psum x1 -> x0, waiting for transfers between devices: 111 us -> none  [body(): lax.psum(shares[0].astype(jnp.bfloat16), 'dp').astype(jnp.float32)]
    unnamed x5 -> x0, waiting for transfers between devices: 44.1 us -> none
    reduce_scatter x1 -> x0, waiting for transfers between devices: 34.7 us -> none  [body(): lax.psum_scatter(gradient_leading.astype(jnp.bfloat16), 'fsdp', scatter_d...]
    dot_general x16 -> x0, matrix products: 27.8 us -> none  [the longest x1 8.77 us: body(): jnp.dot(normalized_input, full_rows, preferred_element_type=jnp.float32)]
  transfers between devices with their start and end apart: 4 -> 0, of which waited for: 4 -> 0; matrix products, arithmetic and copies ran while one was open for 1% -> 0% of each run, Pallas kernels for 0% -> 0%
where the time goes in v1:
time: 128 us
  Pallas kernels  118 us (92%)
  local copies, waits for them, and re-layouts  6.75 us (5%)
  between operations  3.06 us (2%)
    pallas_call x1, Pallas kernels, fused(): pl.pallas_call(kernel, out_shape=(jax.ShapeDtypeStruct((1, 1), F32), jax....  118 us
    unnamed x3, local copies, waits for them, and re-layouts  5.43 us

profile of v1, /device:TPU:1, one launch (start us, length us, event | category | flops | bytes accessed | tf_op | source)
XLA Modules:
  0.0 127.5 jit_solution(7373182672534772425)
XLA Ops:
  1.3 1.3 %reshape.18.gain_ref = f32[1,2560]{1,0:T(1,128)} reshape(f32[2560]{0:T(1024)} %param.12) | data formatting | bytes 20480 | tf_op jit(solution)/shard_map/reshape | solution.py:641
  2.6 2.2 %copy.11.up_hbm = bf16[3072,64]{1,0:T(8,128)(2,1)} copy(bf16[3072,64]{0,1:T(8,128)(2,1)} %param.15) | data formatting | bytes 786432 | tf_op args[7]
  4.7 117.7 %shard_map.103 = (f32[1,1]{1,0:T(1,128)}, f32[320,128]{1,0:T(8,128)}, f32[384,64]{1,0:T(8,128)}) custom-call(s32[1,2]{1,0:T(1,128)} %len_ref.1, s32[1,1]{1,0:T(1,128)S(6)} %copy.15.grp_ref, f32[1,2560]{1,0:T(1,128)} %reshape.18.gain_ref, bf16[256,2560]{1,0:T(8,128)(2,1)} %bitcast.3, bf16[256,2560]{1,0:T(8,128)(2,1)} %bitcast.4, bf16[320,3584]{1,0:T(8,128)(2,1)} %w_hbm.1, ...), custom_call_target="tpu_custom_call" | custom-call | flops 8000000000 | bytes 8000000 | tf_op jit(solution)/shard_map/pallas_call | solution.py:561
  122.5 1.7 %copy.12 = f32[384,64]{0,1:T(8,128)} copy(f32[384,64]{1,0:T(8,128)} %get-tuple-element.11) | data formatting | bytes 196608
  124.8 1.6 %copy.17 = f32[320,128]{1,0:T(8,128)} copy(f32[320,128]{1,0:T(8,128)} %get-tuple-element.16) | data formatting | bytes 327680

commit v2 on v1

--- a/solution.py
+++ b/solution.py
@@ -17,7 +17,10 @@
 SHARD = 320
 HALF = 160
 UNITS = 14
-AHEAD0, AHEAD1, AHEAD2 = 4, 2, 1
+SPLIT_UNITS = 12
+SPLITS = 4
+AHEAD0, AHEAD1, AHEAD2, AHEADZ = 9, 7, 5, 3
+BURST = 2
 
 MESH = pl.DeviceIdType.MESH
 F32 = jnp.float32
@@ -40,25 +43,24 @@
     tgt_hbm,
     w_hbm,
     down_hbm,
-    up_hbm,
+    up_t_hbm,
     loss_ref,
-    ga_ref,
-    gb_ref,
+    fin_ref,
     wbuf,
     hbuf,
     normed,
     normed_t,
     tbuf,
     down,
-    up,
+    up_t,
     lowq,
     lowv,
     low_t,
+    left,
     kbuf,
-    vpol,
-    vref,
+    k_t,
+    vcat,
     mask,
-    sacc,
     dvacc,
     dq_all,
     xsum,
@@ -81,6 +83,8 @@
     y_recv,
     x_send,
     x_recv,
+    z_send,
+    z_recv,
     d_send,
     d_recv,
     q_send,
@@ -163,7 +167,7 @@
     tgt_copy.start()
     down_copy = pltpu.make_async_copy(down_hbm, down, lsem.at[2])
     down_copy.start()
-    up_copy = pltpu.make_async_copy(up_hbm, up, lsem.at[3])
+    up_copy = pltpu.make_async_copy(up_t_hbm, up_t, lsem.at[3])
     up_copy.start()
 
     barrier = pltpu.get_barrier_semaphore()
@@ -214,58 +218,113 @@
         ref = wbuf.at[u, pl.ds(0, n), :]
         remote(ref, ref, y_send.at[kind], y_recv.at[kind, u], on_y(1)).wait_recv()
 
-    def stage0(u):
+    z_par = lax.rem(z, 2)
+
+    def split(u):
+        return (u < SPLIT_UNITS) & (lax.rem(u, 3) < 2)
+
+    def takes(u):
+        return split(u) & (lax.rem(u, 3) != z_par)
+
+    def gives(u):
+        return split(u) & (lax.rem(u, 3) == z_par)
+
+    def wait_own(u):
         ref = wbuf.at[u, rows(own_off, SHARD), :]
         pltpu.make_async_copy(ref, ref, wsem.at[u]).wait()
-        send_y(u, 0, own_off, SHARD, on_y(1))
-        send_y(u, 1, own_off, SHARD, on_y(3))
-        send_x(u, own_off)
-        send_x_back(u, own_off)
+
+    def stage0(u):
+        @pl.when(jnp.logical_not(takes(u)))
+        def _():
+            wait_own(u)
+            send_y(u, 0, own_off, SHARD, on_y(1))
+            send_y(u, 1, own_off, SHARD, on_y(3))
+            send_x(u, own_off)
+            send_x_back(u, own_off)
 
     def stage1(u):
-        wait_y(u, 0, SHARD)
-        off = shard_off(3)
-        send_y(u, 2, off, HALF, on_y(1))
-        send_x(u, off)
-        send_x_back(u, off)
-        wait_y(u, 1, SHARD)
-        off = shard_off(1)
-        send_y(u, 3, off + HALF, HALF, on_y(3))
-        send_x(u, off)
-        send_x_back(u, off)
+        @pl.when(jnp.logical_not(takes(u)))
+        def _():
+            wait_y(u, 0, SHARD)
+            off = shard_off(3)
+            send_y(u, 2, off, HALF, on_y(1))
+            send_x(u, off)
+            send_x_back(u, off)
+            wait_y(u, 1, SHARD)
+            off = shard_off(1)
+            send_y(u, 3, off + HALF, HALF, on_y(3))
+            send_x(u, off)
+            send_x_back(u, off)
 
     def stage2(u):
-        off = shard_off(2)
-        wait_y(u, 2, HALF)
-        send_x(u, off)
-        wait_y(u, 3, HALF)
-        send_x_back(u, off)
-
-    def stage3(u):
+        @pl.when(jnp.logical_not(takes(u)))
+        def _():
+            off = shard_off(2)
+            wait_y(u, 2, HALF)
+            send_x(u, off)
+            wait_y(u, 3, HALF)
+            send_x_back(u, off)
+
+    def wait_x(u):
         ref = wbuf.at[u, pl.ds(0, 8 * HALF), :]
         remote(ref, ref, x_send.at[0], x_recv.at[u], on_x(1)).wait_recv()
 
+    def send_z(u, way, off, n):
+        ref = piece(u, off, n)
+        remote(ref, ref, z_send.at[way], z_recv.at[u], on_z((1, NZ - 1)[way])).start()
+
+    def stage_z(u):
+        @pl.when(gives(u))
+        def _():
+            wait_x(u)
+            for j in range(1, 8):
+                off = SHARD * lax.rem(f + j, 8)
+                if j == 4:
+                    send_z(u, 0, off, HALF)
+                    send_z(u, 1, off + HALF, HALF)
+                else:
+                    send_z(u, 0 if j < 4 else 1, off, SHARD)
+
+    def stage3(u):
+        @pl.when(takes(u))
+        def _():
+            wait_own(u)
+            ref = wbuf.at[u, pl.ds(0, 7 * SHARD), :]
+            remote(ref, ref, z_send.at[0], z_recv.at[u], on_z(1)).wait_recv()
+
+        @pl.when(jnp.logical_not(split(u)))
+        def _():
+            wait_x(u)
+
     def advance(u):
-        @pl.when(u + AHEAD0 < UNITS)
-        def _():
-            stage0(u + AHEAD0)
-
-        @pl.when(u + AHEAD1 < UNITS)
-        def _():
-            stage1(u + AHEAD1)
-
-        @pl.when(u + AHEAD2 < UNITS)
-        def _():
-            stage2(u + AHEAD2)
+        for stage, ahead in (
+            (stage0, AHEAD0),
+            (stage1, AHEAD1),
+            (stage2, AHEAD2),
+            (stage_z, AHEADZ),
+        ):
+
+            @pl.when(u + ahead < UNITS)
+            def _(stage=stage, ahead=ahead):
+                stage(u + ahead)
 
         stage3(u)
 
-    for u in range(AHEAD0):
-        stage0(u)
-
-    meta_copy = remote(
-        meta.at[core], meta.at[core], d_send.at[0], d_recv.at[0], mate
-    )
+    def early(tick):
+        for stage, ahead in (
+            (stage0, AHEAD0),
+            (stage1, AHEAD1),
+            (stage2, AHEAD2),
+            (stage_z, AHEADZ),
+        ):
+            if 0 <= tick + ahead < UNITS:
+                stage(tick + ahead)
+
+    ticks = iter(range(-AHEAD0, 0))
+    for _ in range(BURST):
+        early(next(ticks))
+
+    meta_copy = remote(meta.at[core], meta.at[core], d_send.at[0], d_recv.at[0], mate)
     meta_copy.start()
     tgt_remote = remote(
         tgt_hbm.at[:, lanes(1280 * other, 1280)],
@@ -277,7 +336,7 @@
     tgt_remote.start()
 
     hid_copy.wait()
-    gain = gain_ref[...]
+    gain = gain_ref[...].reshape(1, MODEL)
 
     def norm_block(i, carry):
         values = hbuf[pl.ds(pl.multiple_of(32 * i, 32), 32), :].astype(F32)
@@ -291,6 +350,7 @@
         normed.at[my_rows, :], normed.at[my_rows, :], d_send.at[2], d_recv.at[2], mate
     )
     normed_copy.start()
+    early(next(ticks))
 
     meta_copy.wait()
     cnt[0] = meta[0] + meta[1]
@@ -312,12 +372,10 @@
         cnt[step + 1] = cnt[step] + jnp.sum(buf[...], axis=0)
 
     copies_y = spread(0, NY, on_y, cbuf_y)
-    stage1(0)
-
-    down_copy.wait()
-    up_copy.wait()
-    key_at = lax.broadcasted_iota(jnp.int32, (HEAD, HEAD), 1)
-    query_at = lax.broadcasted_iota(jnp.int32, (HEAD, HEAD), 0)
+    early(next(ticks))
+
+    key_at = lax.broadcasted_iota(jnp.int32, (HEAD, HEAD), 0)
+    query_at = lax.broadcasted_iota(jnp.int32, (HEAD, HEAD), 1)
     for n in range(4):
         length = meta[n // 2, pl.ds(n % 2, 1), :]
         allowed = (key_at <= query_at) & (key_at.astype(F32) < length)
@@ -326,15 +384,17 @@
     tgt_remote.wait()
     for n in range(4):
         length = meta[n // 2, pl.ds(n % 2, 1), :]
-        keep = query_at.astype(F32) < length
+        keep = key_at.astype(F32) < length
         for i in range(10):
             at = (pl.ds(HEAD * n, HEAD), pl.ds(HEAD * i, HEAD))
             tbuf[at] = jnp.where(keep, tbuf[at].astype(F32), F32(0.0)).astype(BF16)
+    early(next(ticks))
 
     gathered(0, copies_y, cbuf_y)
     copies_x = spread(1, NX, on_x, cbuf_x)
-    stage1(1)
-
+
+    down_copy.wait()
+    up_copy.wait()
     normed_copy.wait()
     low = mm(normed[...], down[...])
     lowq[...] = low[:, :RANK].astype(BF16)
@@ -343,49 +403,40 @@
         low_t[:, HEAD * n : HEAD * (n + 1)] = (
             low[HEAD * n : HEAD * (n + 1), :].astype(BF16).astype(F32).T
         )
+    xsum[...] = jnp.zeros_like(xsum)
+    early(next(ticks))
     gathered(1, copies_x, cbuf_x)
     copies_z = spread(2, NZ, on_z, cbuf_z)
-    stage2(0)
-
-    sacc[...] = jnp.zeros_like(sacc)
-    xsum[...] = jnp.zeros_like(xsum)
+    for tick in ticks:
+        early(tick)
 
     def head_step(u, h, i):
         advance(u)
         qi = 5 * h + i
+        block = 10 * core + qi
         base = mm(normed[...], wbuf[u])
-        upq = up[rows(HEAD * (10 * core + qi), HEAD), :]
-        upper = mm_nt(lowq[...], upq)
-        qpol = (base + ADAPT_SCALE * upper).astype(BF16)
+        upq = up_t[:, lanes(HEAD * block, HEAD)]
+        qpol = (base + ADAPT_SCALE * mm(lowq[...], upq)).astype(BF16)
         qref = base.astype(BF16)
-        grads = []
         for n in range(4):
             at = slice(HEAD * n, HEAD * (n + 1))
-            keys = kbuf[h, at, :]
-            values = vpol[h, at, :]
             both = jnp.concatenate([qpol[at], qref[at]], 0)
-            scores = mm_nt(both, keys) * HEAD ** (-0.5)
-            allowed = jnp.concatenate([mask[n], mask[n]], 0) > 0.0
+            scores = mm_nt(kbuf[h, at, :], both) * HEAD ** (-0.5)
+            allowed = jnp.concatenate([mask[n], mask[n]], 1) > 0.0
             expo = jnp.where(allowed, jnp.exp(scores), F32(0.0))
-            probs = expo * (1.0 / jnp.sum(expo, -1, keepdims=True))
-            probs16 = probs.astype(BF16)
-            pol = probs16[:HEAD]
-            att_pol = mm(pol, values).astype(BF16).astype(F32)
-            att_ref = mm(probs16[HEAD:], vref[h, at, :]).astype(BF16).astype(F32)
+            probs = expo * (1.0 / jnp.sum(expo, 0, keepdims=True))
             target = tbuf[at, lanes(HEAD * qi, HEAD)]
-            part = (att_pol - att_ref) * target.astype(F32)
-            sacc[n] += jnp.sum(part.reshape(16, 8, HEAD), axis=0)
-            d_probs = mm_nt(target, values)
-            weighed = probs[:HEAD] * d_probs
-            d_scores = weighed - probs[:HEAD] * jnp.sum(weighed, -1, keepdims=True)
-            d_query = mm(d_scores.astype(BF16), keys).astype(BF16)
-            grads.append(d_query)
-            dvacc[at, :] += mm(probs[:HEAD].T.astype(BF16), target)
-        d_query = jnp.concatenate(grads, 0)
-        block = 10 * core + qi
-        dq_all[block] = d_query
+            d_both = mm_nt(vcat[h, n], target)
+            pol = probs[:, :HEAD]
+            weighed = pol * d_both[:HEAD]
+            token = jnp.sum(weighed, 0, keepdims=True)
+            token_ref = jnp.sum(probs[:, HEAD:] * d_both[HEAD:], 0, keepdims=True)
+            xsum[HEAD : HEAD + 1, at] += token - token_ref
+            d_scores = (weighed - pol * token).astype(BF16)
+            dq_all[block, :, at] = mm(k_t[h, :, at], d_scores).astype(BF16)
+            dvacc[at, :] += mm(pol.astype(BF16), target)
         remote(dq_all.at[block], dq_all.at[block], q_send.at[qi], q_recv.at[qi], mate).start()
-        xsum[0:512, 0:RANK] += mm(d_query, upq)
+        xsum[0:RANK, :] += mm(upq, dq_all[block])
         for j in range(2):
             at = lanes(HEAD * (2 * qi + j), HEAD)
             normed_t[at, :] = normed[:, at].T
@@ -393,12 +444,20 @@
     def group_step(h, carry):
         u = 7 * h
         advance(u)
-        kbuf[h] = mm(normed[...], wbuf[u]).astype(BF16)
+        keys = mm(normed[...], wbuf[u]).astype(BF16)
+        kbuf[h] = keys
+        for n in range(4):
+            at = slice(HEAD * n, HEAD * (n + 1))
+            k_t[h, :, at] = keys[at].astype(F32).T.astype(BF16)
         advance(u + 1)
         base = mm(normed[...], wbuf[u + 1])
-        upv = up[rows(MODEL + HEAD * (2 * core + h), HEAD), :]
-        vref[h] = base.astype(BF16)
-        vpol[h] = (base + ADAPT_SCALE * mm_nt(lowv[...], upv)).astype(BF16)
+        block = 20 + 2 * core + h
+        upv = up_t[:, lanes(HEAD * block, HEAD)]
+        values = (base + ADAPT_SCALE * mm(lowv[...], upv)).astype(BF16)
+        for n in range(4):
+            at = slice(HEAD * n, HEAD * (n + 1))
+            vcat[h, n, 0:HEAD] = values[at]
+            vcat[h, n, HEAD:] = base[at].astype(BF16)
         dvacc[...] = jnp.zeros_like(dvacc)
 
         def inner(i, inner_carry):
@@ -406,19 +465,17 @@
             return inner_carry
 
         lax.fori_loop(0, 5, inner, 0)
-        d_values = dvacc[...].astype(BF16)
-        block = 20 + 2 * core + h
-        dq_all[block] = d_values
+        for n in range(4):
+            at = slice(HEAD * n, HEAD * (n + 1))
+            dq_all[block, :, at] = dvacc[at, :].T.astype(BF16)
         remote(
             dq_all.at[block], dq_all.at[block], q_send.at[10 + h], q_recv.at[10 + h], mate
         ).start()
-        xsum[0:512, RANK:] += mm(d_values, upv)
+        xsum[RANK:HEAD, :] += mm(upv, dq_all[block])
         return carry
 
     lax.fori_loop(0, 2, group_step, 0)
 
-    for n in range(4):
-        xsum[512 + n : 513 + n, :] = jnp.sum(sacc[n], axis=0, keepdims=True)
     x_copy = remote(xsum, xrecv, d_send.at[3], d_recv.at[3], mate)
     x_copy.start()
     gathered(2, copies_z, cbuf_z)
@@ -428,9 +485,9 @@
         weights.append(1.0 / (GROUPS * count))
     x_copy.wait()
 
+    differ = xsum[HEAD : HEAD + 1, :] + xrecv[HEAD : HEAD + 1, :]
     diffs = [
-        jnp.sum(xsum[512 + n : 513 + n, :] + xrecv[512 + n : 513 + n, :], axis=-1, keepdims=True)
-        * MODEL ** (-0.5)
+        jnp.sum(differ[:, HEAD * n : HEAD * (n + 1)], axis=-1, keepdims=True) * MODEL ** (-0.5)
         for n in range(4)
     ]
     coefs = []
@@ -442,49 +499,53 @@
         coefs += [slope, -slope]
         loss_ref[...] = loss if c == 0 else jnp.where(core == 1, loss, loss_ref[...])
 
-    half_lane = lax.broadcasted_iota(jnp.int32, (1, HEAD), 1)
     half_row = lax.broadcasted_iota(jnp.int32, (HEAD, 1), 0)
-    lane_scale = jnp.where(half_lane < RANK, F32(HEAD ** (-0.5)), F32(1.0))
     row_scale = jnp.where(half_row < RANK, F32(HEAD ** (-0.5)), F32(1.0))
     low_parts = []
-    left_parts = []
     for n in range(4):
         at = slice(HEAD * n, HEAD * (n + 1))
-        low_parts.append(((xsum[at, :] + xrecv[at, :]) * (lane_scale * coefs[n])).astype(BF16))
-        low_t[:, at] = low_t[:, at] * (row_scale * coefs[n])
-    d_low = jnp.concatenate(low_parts, 0)
-
-    def share_a(j, carry):
-        left = normed_t[rows(SHARD * j + HALF * core, HALF), :]
-        red[j, 0:HALF, :] = mm(left, d_low).astype(BF16)
-        return carry
-
-    lax.fori_loop(0, 8, share_a, 0)
+        scale = row_scale * coefs[n]
+        low_parts.append(((xsum[0:HEAD, at] + xrecv[0:HEAD, at]) * scale).astype(BF16))
+        low_t[:, at] = low_t[:, at] * scale
+    d_low = jnp.concatenate(low_parts, 1)
+    left[0] = low_t[rows(32 * core, 32), :].astype(BF16)
+    left[1] = low_t[rows(RANK + 32 * core, 32), :].astype(BF16)
 
     def mate_blocks(i, carry):
         @pl.when(i < 10)
         def _():
-            block = 10 * other + i
-            remote(
-                dq_all.at[10 * core + i], dq_all.at[block], q_send.at[i], q_recv.at[i], mate
-            ).wait()
+            mine = dq_all.at[10 * core + i]
+            remote(mine, mine, q_send.at[i], q_recv.at[i], mate).wait()
 
         @pl.when(i >= 10)
         def _():
-            block = 20 + 2 * other + i - 10
-            remote(
-                dq_all.at[20 + 2 * core + i - 10], dq_all.at[block], q_send.at[i], q_recv.at[i], mate
-            ).wait()
+            mine = dq_all.at[20 + 2 * core + i - 10]
+            remote(mine, mine, q_send.at[i], q_recv.at[i], mate).wait()
 
         return carry
 
     lax.fori_loop(0, 12, mate_blocks, 0)
-    left_q = low_t[rows(32 * core, 32), :].astype(BF16)
-    left_v = low_t[rows(RANK + 32 * core, 32), :].astype(BF16)
-    for b in range(24):
-        left = left_q if b < 20 else left_v
-        at = HALF + 32 * (b % 3)
-        red[b // 3, at : at + 32, :] = mm(left, dq_all[b]).astype(BF16)
+
+    copies = []
+    for k in (2, 1, 3, 0):
+        yy = lax.rem(y + k, NY)
+        for q in range(2):
+            j = 2 * yy + q
+            part = normed_t[rows(SHARD * j + HALF * core, HALF), :]
+            red[j, 0:HALF, :] = mm_nt(part, d_low).astype(BF16)
+            for i in range(3):
+                b = 3 * j + i
+                which = (b >= 20).astype(jnp.int32)
+                at = HALF + 32 * i
+                red[j, at : at + 32, :] = mm_nt(left[which], dq_all[b]).astype(BF16)
+        if k:
+            copy = remote(
+                red.at[pl.ds(2 * yy, 2)], ry.at[k - 1], r_send.at[k - 1], r_recv.at[k - 1], on_y(k)
+            )
+            copy.start()
+            copies.append(copy)
+    for copy in copies:
+        copy.wait()
 
     def exchange(step, count, place, source, buf):
         copies = []
@@ -498,7 +559,6 @@
         for copy in copies:
             copy.wait()
 
-    exchange(0, NY, on_y, lambda j: red.at[pl.ds(2 * lax.rem(y + j, NY), 2)], ry)
     total = red[pl.ds(2 * y, 2)].astype(F32)
     for j in range(NY - 1):
         total += ry[j].astype(F32)
@@ -533,27 +593,24 @@
     whole = wbuf.at[0, pl.ds(0, 31 * 16), :]
     remote(whole, whole, g_send.at[0], g_recv.at[0], mate).wait()
 
-    parts = [[], [], []]
-    for c in range(2):
-        ga_ref[HALF * c : HALF * (c + 1), :] = fin[c, 0:HALF, :].astype(F32)
-        for i in range(3):
-            at = HALF + 32 * i
-            parts[i].append(fin[c, at : at + 32, :].astype(F32))
-    for i in range(3):
-        gb_ref[HEAD * i : HEAD * (i + 1), :] = jnp.concatenate(parts[i], 0).T
-
-    whole = wbuf.at[:, pl.ds(0, SHARD), :]
+    fin_ref[...] = fin[...]
+
+    sent = UNITS - SPLITS
+    whole = wbuf.at[pl.ds(0, sent), pl.ds(0, SHARD), :]
     for kind in (0, 1):
         remote(whole, whole, y_send.at[kind], y_recv.at[kind, 0], mate).wait_send()
-    whole = wbuf.at[:, pl.ds(0, HALF), :]
+    whole = wbuf.at[pl.ds(0, sent), pl.ds(0, HALF), :]
     for kind in (2, 3):
         remote(whole, whole, y_send.at[kind], y_recv.at[kind, 0], mate).wait_send()
-    whole = wbuf.at[:, pl.ds(0, 4 * HALF), :]
+    whole = wbuf.at[pl.ds(0, sent), pl.ds(0, 4 * HALF), :]
     for kind in (0, 1):
         remote(whole, whole, x_send.at[kind], x_recv.at[0], mate).wait_send()
-
-
-def fused(lengths, groups, gain, hidden, targets, weight, adapter_down, adapter_up):
+    whole = wbuf.at[pl.ds(0, SPLITS), pl.ds(0, 7 * HALF), :]
+    for way in (0, 1):
+        remote(whole, whole, z_send.at[way], z_recv.at[0], mate).wait_send()
+
+
+def fused(lengths, groups, gain, hidden, targets, weight, adapter_down, adapter_up_t):
     any_spec = pl.BlockSpec(memory_space=pl.ANY)
     smem = pl.BlockSpec(memory_space=pltpu.SMEM)
     vmem = pl.BlockSpec(memory_space=pltpu.VMEM)
@@ -562,11 +619,10 @@
         kernel,
         out_shape=(
             jax.ShapeDtypeStruct((1, 1), F32),
-            jax.ShapeDtypeStruct((SHARD, HEAD), F32),
-            jax.ShapeDtypeStruct((3 * HEAD, RANK), F32),
+            jax.ShapeDtypeStruct((2, 256, HEAD), BF16),
         ),
         in_specs=[smem, smem, vmem, any_spec, any_spec, any_spec, any_spec, any_spec],
-        out_specs=(vmem, vmem, vmem),
+        out_specs=(vmem, vmem),
         scratch_shapes=[
             pltpu.VMEM((UNITS, MODEL, HEAD), BF16),
             pltpu.VMEM((256, MODEL), BF16),
@@ -574,19 +630,19 @@
             pltpu.VMEM((MODEL, 512), BF16),
             pltpu.VMEM((512, 1280), BF16),
             pltpu.VMEM((MODEL, HEAD), BF16),
-            pltpu.VMEM((3072, RANK), BF16),
+            pltpu.VMEM((RANK, 3072), BF16),
             pltpu.VMEM((512, RANK), BF16),
             pltpu.VMEM((512, RANK), BF16),
             pltpu.VMEM((HEAD, 512), F32),
+            pltpu.VMEM((2, 32, 512), BF16),
             pltpu.VMEM((2, 512, HEAD), BF16),
-            pltpu.VMEM((2, 512, HEAD), BF16),
-            pltpu.VMEM((2, 512, HEAD), BF16),
+            pltpu.VMEM((2, HEAD, 512), BF16),
+            pltpu.VMEM((2, 4, 256, HEAD), BF16),
             pltpu.VMEM((4, HEAD, HEAD), F32),
-            pltpu.VMEM((4, 8, HEAD), F32),
             pltpu.VMEM((512, HEAD), F32),
-            pltpu.VMEM((24, 512, HEAD), BF16),
-            pltpu.VMEM((520, HEAD), F32),
-            pltpu.VMEM((520, HEAD), F32),
+            pltpu.VMEM((24, HEAD, 512), BF16),
+            pltpu.VMEM((136, 512), F32),
+            pltpu.VMEM((136, 512), F32),
             pltpu.VMEM((2, 8, HEAD), F32),
             pltpu.VMEM((4, 8, HEAD), F32),
             pltpu.VMEM((NY - 1, 8, HEAD), F32),
@@ -603,6 +659,8 @@
             dma((4,)),
             dma((4,)),
             dma((4, UNITS)),
+            dma((2,)),
+            dma((UNITS,)),
             dma((2,)),
             dma((UNITS,)),
             dma((4,)),
@@ -622,7 +680,30 @@
         cost_estimate=pl.CostEstimate(
             flops=8_000_000_000, bytes_accessed=8_000_000, transcendentals=1_400_000
         ),
-    )(lengths, groups, gain, hidden, targets, weight, adapter_down, adapter_up)
+    )(lengths, groups, gain, hidden, targets, weight, adapter_down, adapter_up_t)
+
+
+def finish_kernel(fin_ref, ga_ref, gb_t_ref):
+    for c in range(2):
+        ga_ref[HALF * c : HALF * (c + 1), :] = fin_ref[c, 0:HALF, :].astype(F32)
+        for i in range(3):
+            at = HALF + 32 * i
+            gb_t_ref[32 * c : 32 * (c + 1), HEAD * i : HEAD * (i + 1)] = fin_ref[
+                c, at : at + 32, :
+            ].astype(F32)
+
+
+def finish(fin):
+    vmem = pl.BlockSpec(memory_space=pltpu.VMEM)
+    return pl.pallas_call(
+        finish_kernel,
+        out_shape=(
+            jax.ShapeDtypeStruct((SHARD, HEAD), F32),
+            jax.ShapeDtypeStruct((RANK, 3 * HEAD), F32),
+        ),
+        in_specs=[vmem],
+        out_specs=(vmem, vmem),
+    )(fin)
 
 
 def body(
@@ -635,17 +716,18 @@
     adapter_down,
     adapter_up,
 ):
-    losses, grad_a, grad_b = fused(
+    losses, fin = fused(
         lengths,
         prompt_group_index,
-        input_norm_gain.reshape(1, MODEL),
+        input_norm_gain,
         hidden.reshape(256, MODEL),
         targets.reshape(256, MODEL),
         frozen_weight,
         adapter_down,
-        adapter_up,
+        adapter_up.T,
     )
-    return (losses.reshape(1), grad_a, grad_b)
+    grad_a, grad_b_t = finish(fin)
+    return (losses.reshape(1), grad_a, grad_b_t.T)
 
 
 def solution(mesh):

time: 128 us -> 102 us (0.80)
  Pallas kernels: 118 us -> 98.3 us
  local copies, waits for them, and re-layouts: 6.75 us -> 0 us
    pallas_call x1, Pallas kernels: 118 us -> 96.7 us  [fused(): pl.pallas_call(kernel, out_shape=(jax.ShapeDtypeStruct((1, 1), F32), jax....]
    unnamed x3 -> x0, local copies, waits for them, and re-layouts: 5.43 us -> none
    pallas_call x0 -> x1, Pallas kernels: none -> 1.62 us  [finish(): pl.pallas_call(finish_kernel, out_shape=(jax.ShapeDtypeStruct((SHARD, HEA...]
    reshape x1 -> x0, local copies, waits for them, and re-layouts: 1.31 us -> none  [body(): input_norm_gain.reshape(1, MODEL)]
where the time goes in v2:
time: 102 us; the launch traced here: 101 us
  Pallas kernels  98.3 us (96%)
  between operations  3.04 us (3%)
    pallas_call x1, Pallas kernels, fused(): pl.pallas_call(kernel, out_shape=(jax.ShapeDtypeStruct((1, 1), F32), jax....  96.7 us

profile of v2, /device:TPU:1, one launch (start us, length us, event | category | flops | bytes accessed | tf_op | source)
XLA Modules:
  0.0 101.4 jit_solution(16873465308128529456)
XLA Ops:
  1.3 96.7 %shard_map.103 = (f32[1,1]{1,0:T(1,128)}, bf16[2,256,128]{2,1,0:T(8,128)(2,1)}) custom-call(s32[1,2]{1,0:T(1,128)} %len_ref.1, s32[1,1]{1,0:T(1,128)S(6)} %copy.12.grp_ref, f32[2560]{0:T(1024)} %gain_ref.1, bf16[256,2560]{1,0:T(8,128)(2,1)} %bitcast.5, bf16[256,2560]{1,0:T(8,128)(2,1)} %bitcast.6, bf16[320,3584]{1,0:T(8,128)(2,1)} %w_hbm.1, ...), custom_call_target="tpu_custom_call" | custom-call | flops 8000000000 | bytes 8000000 | tf_op jit(solution)/shard_map/pallas_call | solution.py:618
  98.0 1.6 %shard_map.104 = (f32[320,128]{1,0:T(8,128)}, f32[64,384]{1,0:T(8,128)}) custom-call(bf16[2,256,128]{2,1,0:T(8,128)(2,1)} %get-tuple-element.8.fin_ref), custom_call_target="tpu_custom_call" | custom-call | tf_op jit(solution)/shard_map/pallas_call | solution.py:698

commit v3 on v2

--- a/solution.py
+++ b/solution.py
@@ -18,9 +18,10 @@
 HALF = 160
 UNITS = 14
 SPLIT_UNITS = 12
-SPLITS = 4
+SPLITS = SPLIT_UNITS // 3
 AHEAD0, AHEAD1, AHEAD2, AHEADZ = 9, 7, 5, 3
 BURST = 2
+COUNT_UNIT = 12
 
 MESH = pl.DeviceIdType.MESH
 F32 = jnp.float32
@@ -67,14 +68,11 @@
     xrecv,
     meta,
     cnt,
-    cbuf_y,
-    cbuf_x,
+    cbuf_p,
     cbuf_z,
     red,
-    red1,
     red2,
-    ry,
-    rx,
+    rp,
     rz,
     fin,
     wsem,
@@ -98,24 +96,31 @@
 ):
     d = lax.axis_index("dp")
     f = lax.axis_index("fsdp")
-    core = lax.rem(d, 2)
-    xh = lax.rem(lax.div(d, 2), 2)
-    z = lax.div(d, 4)
-    par = lax.rem(f, 2)
-    y = lax.div(f, 2)
+    core = d & 1
+    xh = (d >> 1) & 1
+    z = d >> 2
+    par = f & 1
+    y = f >> 1
     x = 2 * xh + par
 
-    def dev(zz, xx, yy, cc):
-        return (zz * 4 + lax.div(xx, 2) * 2 + cc, yy * 2 + lax.rem(xx, 2))
+    def dev(zz, xx, yy):
+        return (zz * 4 + (xx & 2) + core, yy * 2 + (xx & 1))
+
+    to_y = [dev(z, x, (y + j) & 3) for j in range(NY)]
+    to_x = [dev(z, (x + j) & 3, y) for j in range(NX)]
+    to_z = [((d + 4 * j) & 31, f) for j in range(NZ)]
+
+    def in_plane(jy, jx):
+        return dev(z, (x + jx) & 3, (y + jy) & 3)
 
     def on_y(j):
-        return dev(z, x, lax.rem(y + j, NY), core)
+        return to_y[j]
 
     def on_x(j):
-        return dev(z, lax.rem(x + j, NX), y, core)
+        return to_x[j]
 
     def on_z(j):
-        return dev(lax.rem(z + j, NZ), x, y, core)
+        return to_z[j]
 
     other = 1 - core
     mate = (d + 1 - 2 * core, f)
@@ -132,8 +137,11 @@
 
     own_off = SHARD * f
 
+    y_off = [SHARD * (2 * ((y + j) & 3) + par) for j in range(NY)]
+    f_off = [SHARD * ((f + j) & 7) for j in range(8)]
+
     def shard_off(j):
-        return SHARD * (2 * lax.rem(y + j, NY) + par)
+        return y_off[j]
 
     def rows(off, n):
         return pl.ds(pl.multiple_of(off, 32), n)
@@ -172,17 +180,8 @@
 
     barrier = pltpu.get_barrier_semaphore()
 
-    def greet(j, carry):
-        pl.semaphore_signal(
-            barrier, inc=1, device_id=(lax.rem(d + j, 32), f), device_id_type=MESH
-        )
-        return carry
-
-    for j in (1, 2, 3):
-        pl.semaphore_signal(barrier, inc=1, device_id=on_y(j), device_id_type=MESH)
-    for j in (1, 3):
-        pl.semaphore_signal(barrier, inc=1, device_id=on_x(j), device_id_type=MESH)
-    lax.fori_loop(1, 32, greet, 0)
+    for target in (on_y(1), on_y(3), on_x(1), on_x(3), on_z(1), on_z(7), mate):
+        pl.semaphore_signal(barrier, inc=1, device_id=target, device_id_type=MESH)
 
     lane = lax.broadcasted_iota(jnp.int32, (8, HEAD), 1)
     row = lax.broadcasted_iota(jnp.int32, (8, HEAD), 0)
@@ -197,7 +196,7 @@
     )
     meta[pl.ds(core, 1)] = meta_own[None]
 
-    pl.semaphore_wait(barrier, 36)
+    pl.semaphore_wait(barrier, 7)
 
     def piece(u, off, n):
         return wbuf.at[u, rows(off, n), :]
@@ -218,7 +217,7 @@
         ref = wbuf.at[u, pl.ds(0, n), :]
         remote(ref, ref, y_send.at[kind], y_recv.at[kind, u], on_y(1)).wait_recv()
 
-    z_par = lax.rem(z, 2)
+    z_par = z & 1
 
     def split(u):
         return (u < SPLIT_UNITS) & (lax.rem(u, 3) < 2)
@@ -278,7 +277,7 @@
         def _():
             wait_x(u)
             for j in range(1, 8):
-                off = SHARD * lax.rem(f + j, 8)
+                off = f_off[j]
                 if j == 4:
                     send_z(u, 0, off, HALF)
                     send_z(u, 1, off + HALF, HALF)
@@ -355,23 +354,25 @@
     meta_copy.wait()
     cnt[0] = meta[0] + meta[1]
 
-    def spread(step, count, place, buf):
-        copies = []
-        base = (0, 3, 6)[step]
-        for j in range(1, count):
-            copy = remote(
-                cnt.at[step], buf.at[j - 1], c_send.at[base + j - 1], c_recv.at[base + j - 1], place(j)
+    def plane_counts():
+        return [
+            remote(
+                cnt.at[0], cbuf_p.at[j - 1], c_send.at[j - 1], c_recv.at[j - 1], in_plane(j >> 2, j & 3)
             )
-            copy.start()
-            copies.append(copy)
-        return copies
+            for j in range(1, NX * NY)
+        ]
+
+    def z_counts():
+        return [
+            remote(cnt.at[1], cbuf_z.at[j - 1], c_send.at[14 + j], c_recv.at[14 + j], on_z(j))
+            for j in range(1, NZ)
+        ]
 
     def gathered(step, copies, buf):
         for copy in copies:
             copy.wait()
         cnt[step + 1] = cnt[step] + jnp.sum(buf[...], axis=0)
 
-    copies_y = spread(0, NY, on_y, cbuf_y)
     early(next(ticks))
 
     key_at = lax.broadcasted_iota(jnp.int32, (HEAD, HEAD), 0)
@@ -390,9 +391,6 @@
             tbuf[at] = jnp.where(keep, tbuf[at].astype(F32), F32(0.0)).astype(BF16)
     early(next(ticks))
 
-    gathered(0, copies_y, cbuf_y)
-    copies_x = spread(1, NX, on_x, cbuf_x)
-
     down_copy.wait()
     up_copy.wait()
     normed_copy.wait()
@@ -405,10 +403,10 @@
         )
     xsum[...] = jnp.zeros_like(xsum)
     early(next(ticks))
-    gathered(1, copies_x, cbuf_x)
-    copies_z = spread(2, NZ, on_z, cbuf_z)
     for tick in ticks:
         early(tick)
+    for copy in plane_counts():
+        copy.start()
 
     def head_step(u, h, i):
         advance(u)
@@ -462,6 +460,13 @@
 
         def inner(i, inner_carry):
             head_step(u + 2 + i, h, i)
+
+            @pl.when(u + 2 + i == COUNT_UNIT)
+            def _():
+                gathered(0, plane_counts(), cbuf_p)
+                for copy in z_counts():
+                    copy.start()
+
             return inner_carry
 
         lax.fori_loop(0, 5, inner, 0)
@@ -478,10 +483,10 @@
 
     x_copy = remote(xsum, xrecv, d_send.at[3], d_recv.at[3], mate)
     x_copy.start()
-    gathered(2, copies_z, cbuf_z)
+    gathered(1, z_counts(), cbuf_z)
     weights = []
     for c in range(2):
-        count = jnp.sum(cnt[3, 2:3, :] * meta[c, 2:3, :], axis=-1, keepdims=True)
+        count = jnp.sum(cnt[2, 2:3, :] * meta[c, 2:3, :], axis=-1, keepdims=True)
         weights.append(1.0 / (GROUPS * count))
     x_copy.wait()
 
@@ -527,10 +532,11 @@
     lax.fori_loop(0, 12, mate_blocks, 0)
 
     copies = []
-    for k in (2, 1, 3, 0):
-        yy = lax.rem(y + k, NY)
-        for q in range(2):
-            j = 2 * yy + q
+    for jy in (2, 1, 3, 0):
+        yy = (y + jy) & 3
+        for jp in (1, 0):
+            pp = par ^ jp
+            j = 2 * yy + pp
             part = normed_t[rows(SHARD * j + HALF * core, HALF), :]
             red[j, 0:HALF, :] = mm_nt(part, d_low).astype(BF16)
             for i in range(3):
@@ -538,46 +544,38 @@
                 which = (b >= 20).astype(jnp.int32)
                 at = HALF + 32 * i
                 red[j, at : at + 32, :] = mm_nt(left[which], dq_all[b]).astype(BF16)
-        if k:
-            copy = remote(
-                red.at[pl.ds(2 * yy, 2)], ry.at[k - 1], r_send.at[k - 1], r_recv.at[k - 1], on_y(k)
-            )
-            copy.start()
-            copies.append(copy)
+            for jx in (jp + 2, jp):
+                slot = 4 * jy + jx - 1
+                if slot < 0:
+                    continue
+                xx = (x + jx) & 3
+                copy = remote(
+                    red.at[j, rows(HEAD * (xx >> 1), HEAD), :],
+                    rp.at[slot],
+                    r_send.at[slot],
+                    r_recv.at[slot],
+                    in_plane(jy, jx),
+                )
+                copy.start()
+                copies.append(copy)
     for copy in copies:
         copy.wait()
 
-    def exchange(step, count, place, source, buf):
-        copies = []
-        base = (0, 3, 6)[step]
-        for j in range(1, count):
-            copy = remote(
-                source(j), buf.at[j - 1], r_send.at[base + j - 1], r_recv.at[base + j - 1], place(j)
-            )
-            copy.start()
-            copies.append(copy)
-        for copy in copies:
-            copy.wait()
-
-    total = red[pl.ds(2 * y, 2)].astype(F32)
-    for j in range(NY - 1):
-        total += ry[j].astype(F32)
-    red1[...] = total.astype(BF16)
-
-    def x_part(j):
-        xx = lax.rem(x + j, NX)
-        return red1.at[lax.rem(xx, 2), rows(HEAD * lax.div(xx, 2), HEAD), :]
-
-    exchange(1, NX, on_x, x_part, rx)
-    total = red1[par, rows(HEAD * xh, HEAD), :].astype(F32)
-    for j in range(NX - 1):
-        total += rx[j].astype(F32)
+    total = red[f, rows(HEAD * xh, HEAD), :].astype(F32)
+    for j in range(NX * NY - 1):
+        total += rp[j].astype(F32)
     red2[...] = total.astype(BF16)
 
     def z_part(j):
-        return red2.at[pl.ds(pl.multiple_of(16 * lax.rem(z + j, NZ), 16), 16), :]
-
-    exchange(2, NZ, on_z, z_part, rz)
+        return red2.at[pl.ds(pl.multiple_of(16 * ((z + j) & 7), 16), 16), :]
+
+    copies = []
+    for j in range(1, NZ):
+        copy = remote(z_part(j), rz.at[j - 1], r_send.at[14 + j], r_recv.at[14 + j], on_z(j))
+        copy.start()
+        copies.append(copy)
+    for copy in copies:
+        copy.wait()
     total = red2[pl.ds(pl.multiple_of(16 * z, 16), 16), :].astype(F32)
     for j in range(NZ - 1):
         total += rz[j].astype(F32)
@@ -586,7 +584,7 @@
 
     def hand_out(j, carry):
         ref = fin.at[core, mine, :]
-        remote(ref, ref, g_send.at[0], g_recv.at[0], (lax.rem(d + j, 32), f)).start()
+        remote(ref, ref, g_send.at[0], g_recv.at[0], ((d + j) & 31, f)).start()
         return carry
 
     lax.fori_loop(1, 32, hand_out, 0)
@@ -644,15 +642,12 @@
             pltpu.VMEM((136, 512), F32),
             pltpu.VMEM((136, 512), F32),
             pltpu.VMEM((2, 8, HEAD), F32),
-            pltpu.VMEM((4, 8, HEAD), F32),
-            pltpu.VMEM((NY - 1, 8, HEAD), F32),
-            pltpu.VMEM((NX - 1, 8, HEAD), F32),
+            pltpu.VMEM((3, 8, HEAD), F32),
+            pltpu.VMEM((NX * NY - 1, 8, HEAD), F32),
             pltpu.VMEM((NZ - 1, 8, HEAD), F32),
             pltpu.VMEM((8, 256, HEAD), BF16),
-            pltpu.VMEM((2, 256, HEAD), BF16),
             pltpu.VMEM((HEAD, HEAD), BF16),
-            pltpu.VMEM((NY - 1, 2, 256, HEAD), BF16),
-            pltpu.VMEM((NX - 1, HEAD, HEAD), BF16),
+            pltpu.VMEM((NX * NY - 1, HEAD, HEAD), BF16),
             pltpu.VMEM((NZ - 1, 16, HEAD), BF16),
             pltpu.VMEM((2, 256, HEAD), BF16),
             dma((UNITS,)),
@@ -667,10 +662,10 @@
             dma((4,)),
             dma((12,)),
             dma((12,)),
-            dma((13,)),
-            dma((13,)),
-            dma((13,)),
-            dma((13,)),
+            dma((22,)),
+            dma((22,)),
+            dma((22,)),
+            dma((22,)),
             dma((1,)),
             dma((1,)),
         ],

time: 102 us -> 95 us (0.931)
  Pallas kernels: 98.3 us -> 91.8 us
    pallas_call x1, Pallas kernels: 96.7 us -> 90.2 us  [fused(): pl.pallas_call(kernel, out_shape=(jax.ShapeDtypeStruct((1, 1), F32), jax....]
where the time goes in v3:
time: 95 us; the launch traced here: 94.9 us
  Pallas kernels  91.8 us (97%)
  between operations  3.04 us (3%)
    pallas_call x1, Pallas kernels, fused(): pl.pallas_call(kernel, out_shape=(jax.ShapeDtypeStruct((1, 1), F32), jax....  90.2 us

profile of v3, /device:TPU:1, one launch (start us, length us, event | category | flops | bytes accessed | tf_op | source)
XLA Modules:
  0.0 94.9 jit_solution(87726656961069928)
XLA Ops:
  1.3 90.2 %shard_map.103 = (f32[1,1]{1,0:T(1,128)}, bf16[2,256,128]{2,1,0:T(8,128)(2,1)}) custom-call(s32[1,2]{1,0:T(1,128)} %len_ref.1, s32[1,1]{1,0:T(1,128)S(6)} %copy.12.grp_ref, f32[2560]{0:T(1024)} %gain_ref.1, bf16[256,2560]{1,0:T(8,128)(2,1)} %bitcast.5, bf16[256,2560]{1,0:T(8,128)(2,1)} %bitcast.6, bf16[320,3584]{1,0:T(8,128)(2,1)} %w_hbm.1, ...), custom_call_target="tpu_custom_call" | custom-call | flops 8000000000 | bytes 8000000 | tf_op jit(solution)/shard_map/pallas_call | solution.py:616
  91.5 1.6 %shard_map.104 = (f32[320,128]{1,0:T(8,128)}, f32[64,384]{1,0:T(8,128)}) custom-call(bf16[2,256,128]{2,1,0:T(8,128)(2,1)} %get-tuple-element.8.fin_ref), custom_call_target="tpu_custom_call" | custom-call | tf_op jit(solution)/shard_map/pallas_call | solution.py:693

commit v4 on v3

--- a/solution.py
+++ b/solution.py
@@ -570,7 +570,7 @@
         return red2.at[pl.ds(pl.multiple_of(16 * ((z + j) & 7), 16), 16), :]
 
     copies = []
-    for j in range(1, NZ):
+    for j in (4, 3, 5, 2, 6, 1, 7):
         copy = remote(z_part(j), rz.at[j - 1], r_send.at[14 + j], r_recv.at[14 + j], on_z(j))
         copy.start()
         copies.append(copy)
@@ -582,12 +582,9 @@
     mine = pl.ds(pl.multiple_of(HEAD * xh + 16 * z, 16), 16)
     fin[core, mine, :] = total.astype(BF16)
 
-    def hand_out(j, carry):
-        ref = fin.at[core, mine, :]
-        remote(ref, ref, g_send.at[0], g_recv.at[0], ((d + j) & 31, f)).start()
-        return carry
-
-    lax.fori_loop(1, 32, hand_out, 0)
+    final = fin.at[core, mine, :]
+    for j in sorted(range(1, 32), key=lambda j: abs(j - 16)):
+        remote(final, final, g_send.at[0], g_recv.at[0], ((d + j) & 31, f)).start()
     whole = wbuf.at[0, pl.ds(0, 31 * 16), :]
     remote(whole, whole, g_send.at[0], g_recv.at[0], mate).wait()
 

time: 95 us -> 94.1 us (level)
  no operation moved by 1% of the time
where the time goes in v4:
time: 94.1 us; the launch traced here: 94 us
  Pallas kernels  90.9 us (97%)
  between operations  3.04 us (3%)
    pallas_call x1, Pallas kernels, fused(): pl.pallas_call(kernel, out_shape=(jax.ShapeDtypeStruct((1, 1), F32), jax....  89.3 us

profile of v4, /device:TPU:1, one launch (start us, length us, event | category | flops | bytes accessed | tf_op | source)
XLA Modules:
  0.0 94.0 jit_solution(16034261611001608949)
XLA Ops:
  1.3 89.3 %shard_map.103 = (f32[1,1]{1,0:T(1,128)}, bf16[2,256,128]{2,1,0:T(8,128)(2,1)}) custom-call(s32[1,2]{1,0:T(1,128)} %len_ref.1, s32[1,1]{1,0:T(1,128)S(6)} %copy.12.grp_ref, f32[2560]{0:T(1024)} %gain_ref.1, bf16[256,2560]{1,0:T(8,128)(2,1)} %bitcast.5, bf16[256,2560]{1,0:T(8,128)(2,1)} %bitcast.6, bf16[320,3584]{1,0:T(8,128)(2,1)} %w_hbm.1, ...), custom_call_target="tpu_custom_call" | custom-call | flops 8000000000 | bytes 8000000 | tf_op jit(solution)/shard_map/pallas_call | solution.py:613
  90.6 1.6 %shard_map.104 = (f32[320,128]{1,0:T(8,128)}, f32[64,384]{1,0:T(8,128)}) custom-call(bf16[2,256,128]{2,1,0:T(8,128)(2,1)} %get-tuple-element.8.fin_ref), custom_call_target="tpu_custom_call" | custom-call | tf_op jit(solution)/shard_map/pallas_call | solution.py:690
